TPU v7x, 256 devices: a whole 4x4x8 slice. The times are simulated.
256 devices in a mesh: cell: 32 (over x, y, core), mem: 8 (over z).
Axes of the slice: x: 4, y: 4, z: 8, core: 2. Of those that a mesh axis runs over, the one named last changes fastest.
Arguments:
- ensemble: float32 [256, 65536], P('mem', 'cell'), may hold values from -6 to 6
- weights: float32 [4, 128, 512], replicated, may hold values from -0.25 to 0.25
- blocks: int32 [4, 128, 8], replicated, may hold values from 0 to 1023
- owner_ids: int32 [4], replicated, may hold values from 0 to 31
- counts: int32 [4], replicated, may hold values from 64 to 128, as said below
- obs_values: float32 [128, 128], P('cell'), may hold values from -8 to 8
- obs_error: float32 [128, 128], P('cell'), may hold values from 0.3 to 3
Outputs:
- posterior: float32 [256, 65536], P('mem', 'cell')
Inputs may be any that keep to these rules, and one draw needn't show every extreme that they name: Observations o < counts[b] of batch b are live; one batch has all 128 live, another 128 // 2.
All inputs are finite; a program needn't handle non-finite values.
Results may differ from a plain program's by a relative error of at most 0.00015.
Values sent between devices are 32-bit elements; how exact they have to be, the bound alone decides.
No kernel may reach another device: no remote copies, remote signals or barrier semaphores. Data moves between devices by JAX's collectives and lax.ppermute only.
A program may use at most 64 MiB of HBM per device.

v0:
```python
import jax
import jax.numpy as jnp
from jax import lax
from jax.experimental import pallas as pl
from jax.experimental.pallas import tpu as pltpu
from jax.sharding import PartitionSpec as P

MEMBERS = 256
NOBS = 128
NB = 4
FB = 8
BLK = 64
LANES = 128
SUB = 8
HIGH = lax.Precision.HIGHEST
HBM = pl.BlockSpec(memory_space=pltpu.HBM)
VMEM = pl.BlockSpec(memory_space=pltpu.VMEM)
SMEM = pl.BlockSpec(memory_space=pltpu.SMEM)


def dot(a, b, ca=1, cb=0):
    return lax.dot_general(a, b, (((ca,), (cb,)), ((), ())), precision=HIGH)


def split(array):
    high = array.astype(jnp.bfloat16)
    return high, (array - high.astype(jnp.float32)).astype(jnp.bfloat16)


def priors_kernel(owners_ref, state_ref, weights_ref, blocks_ref, values_ref, error_ref, out_ref):
    members, cells = state_ref.shape
    chunks = cells // LANES
    fit = LANES // members
    rows = NB * NOBS
    cell = lax.axis_index("cell")
    half = lax.broadcasted_iota(jnp.int32, (rows, LANES), 1) // BLK
    place = lax.broadcasted_iota(jnp.int32, (rows, LANES), 1) // members
    state = jnp.concatenate([state_ref[:, g * LANES : (g + 1) * LANES] for g in range(chunks)], 0)
    high, low = split(state.T)
    right = jnp.concatenate([high, high, low, low], 0)
    weights = weights_ref[...].reshape(rows, FB * BLK)
    first = cell * (cells // BLK)
    block = jnp.concatenate([(blocks_ref[b] - first).T for b in range(NB)], 0)
    total = [jnp.zeros((rows, LANES), jnp.float32) for _ in range(chunks // fit)]
    for f in range(FB):
        pair = weights[:, (f // 2) * LANES : (f // 2 + 1) * LANES]
        both = jnp.where(half == f % 2, pair, pltpu.roll(pair, BLK, 1))
        index = jnp.broadcast_to(block[:, f : f + 1], (rows, LANES))
        high, low = split(jnp.where((index & 1) == half, both, 0.0))
        left = jnp.concatenate([high, low, high, low], 1)
        product = jnp.dot(left, right, preferred_element_type=jnp.float32)
        group = (index >> 1) - place
        for c in range(chunks // fit):
            total[c] = total[c] + jnp.where(group == c * fit, product[:, c * LANES : (c + 1) * LANES], 0.0)
    kept = tree(total)
    shift = LANES // 2
    while shift >= members:
        kept = kept + pltpu.roll(kept, shift, 1)
        shift //= 2
    for b in range(NB):
        at = slice(b * NOBS, (b + 1) * NOBS)
        mine = owners_ref[b] == cell
        out_ref[:members, at] = kept[at].T[:members]
        out_ref[members : members + 1, at] = jnp.where(mine, values_ref[b : b + 1, :], 0.0)
        out_ref[members + 1 : members + 2, at] = jnp.where(mine, error_ref[b : b + 1, :], 0.0)
    out_ref[members + 2 :, :] = jnp.zeros((SUB - 2, rows), jnp.float32)


def local_priors(owners, state, weights, blocks, values, error):
    members = state.shape[0]
    return pl.pallas_call(
        priors_kernel,
        out_shape=jax.ShapeDtypeStruct((members + SUB, NB * NOBS), jnp.float32),
        in_specs=[SMEM] + [VMEM] * 5,
        out_specs=VMEM,
        compiler_params=pltpu.CompilerParams(vmem_limit_bytes=60 << 20),
        name="priors",
    )(owners, state, weights, blocks.transpose(0, 2, 1), values, error)


def spread(tile, s):
    return jnp.broadcast_to(tile[s : s + 1, :], (SUB, LANES))


def tree(terms):
    while len(terms) > 1:
        terms = [a + b for a, b in zip(terms[::2], terms[1::2])] + terms[len(terms) & ~1 :]
    return terms[0]


def split3(a):
    h = a.astype(jnp.bfloat16)
    rest = a - h.astype(jnp.float32)
    m = rest.astype(jnp.bfloat16)
    return h, m, (rest - m.astype(jnp.float32)).astype(jnp.bfloat16)


def eliminate(cov, noise):
    tiles = NOBS // SUB
    sub = lax.broadcasted_iota(jnp.int32, (SUB, LANES), 0)
    lane = lax.broadcasted_iota(jnp.int32, (SUB, LANES), 1)
    noise_cols = jnp.broadcast_to(noise, (NOBS, LANES)).T
    r = [cov[i * SUB : (i + 1) * SUB, :] for i in range(tiles)]
    z = [jnp.where(lane == sub + i * SUB, 1.0, 0.0) for i in range(tiles)]
    y = list(z)
    for k in range(tiles):
        rk, zk, yk = r[k], z[k], y[k]
        cols = {
            i: [jnp.broadcast_to(r[i][:, k * SUB + j : k * SUB + j + 1], (SUB, LANES)) for j in range(SUB)]
            for i in range(k, min(tiles, k + 1 + 1))
        }
        diag = cols.pop(k)
        zero = jnp.zeros((SUB, LANES), jnp.float32)
        root, length, z[k] = zero, zero, zero
        upper = [zero] * SUB
        lower = []
        for j in range(0, SUB, 2):
            one, two = sub == j, sub == j + 1
            a, b, d = spread(diag[j], j), spread(diag[j], j + 1), spread(diag[j + 1], j + 1)
            det = a * d - b * b
            recip = 1.0 / det
            root_a = lax.rsqrt(a)
            ratio = b * (root_a * root_a)
            root_b = a * root_a * lax.rsqrt(det)
            length_b = det * (root_a * root_a) * root_b
            root = jnp.where(one, root_a, jnp.where(two, root_b, root))
            length = jnp.where(one, a * root_a, jnp.where(two, length_b, length))
            lower.append(jnp.where(sub > j, diag[j] * root_a, 0.0))
            lower.append(jnp.where(sub > j + 1, (diag[j + 1] - diag[j] * ratio) * root_b, 0.0))
            z[k] = jnp.where(one, zk * root_a, jnp.where(two, (zk - ratio * spread(zk, j)) * root_b, z[k]))
            if k == tiles - 1 and j == SUB - 2:
                continue
            upper[j + 1] = jnp.where(one, b * root_a, upper[j + 1])
            for m in range(j + 2, SUB):
                second = (diag[m] - ratio * spread(diag[m], j)) * root_b
                upper[m] = jnp.where(one, diag[m] * root_a, jnp.where(two, second, upper[m]))
            left = jnp.where(one, -1.0, jnp.where(two, 0.0, diag[j]))
            right = jnp.where(two, -1.0, jnp.where(one, 0.0, diag[j + 1]))

            def reduce(v):
                p, q = spread(v, j), spread(v, j + 1)
                return jnp.where(one | two, 0.0, v) - (left * (d * p - b * q) + right * (a * q - b * p)) * recip

            for m in range(j + 2, SUB):
                diag[m] = reduce(diag[m])
            rk, zk = reduce(rk), reduce(zk)
        shifted = 1.0 / (length + noise_cols[k * SUB : (k + 1) * SUB, :])
        for j in range(SUB - 1):
            yk = yk - lower[j] * (spread(yk, j) * spread(shifted, j))
        y[k] = yk * shifted
        if k == tiles - 1:
            break
        q, qz, qy = rk, zk, y[k]
        for m in range(SUB - 1, 0, -1):
            qy = qy - upper[m] * (spread(qy, m) * spread(root, m))
        qy = qy * root
        rows = [[spread(v, j) for j in range(SUB)] for v in (q, qz, qy)]
        for i in cols:
            r[i] = r[i] - tree([c * w for c, w in zip(cols[i], rows[0])])
            z[i] = z[i] - tree([c * w for c, w in zip(cols[i], rows[1])])
            y[i] = y[i] - tree([c * w for c, w in zip(cols[i], rows[2])])
        first = k + 1 + 1
        if first < tiles:
            far = jnp.concatenate(r[first:], 0)[:, k * SUB : (k + 1) * SUB]
            change = jnp.concatenate([q, qz, qy], 1)
            f0, f1, f2 = split3(far)
            c0, c1, c2 = split3(change)
            left = jnp.concatenate([f0, f1, f0, f1, f2, f0], 1)
            right = jnp.concatenate([c0, c0, c1, c1, c0, c2], 0)
            change = jnp.dot(left, right, preferred_element_type=jnp.float32)
            for i in range(first, tiles):
                part = change[(i - first) * SUB : (i - first + 1) * SUB]
                r[i] = r[i] - part[:, :LANES]
                z[i] = z[i] - part[:, LANES : 2 * LANES]
                y[i] = y[i] - part[:, 2 * LANES :]
    return jnp.concatenate(z, 0), jnp.concatenate(y, 0)


def analysis_kernel(counts_ref, obs_ref, *refs):
    members = MEMBERS // 8
    parts, out_ref, state = refs[:8], refs[8], refs[9]
    for k in range(8):
        state[k * members : (k + 1) * members, : NB * NOBS] = parts[k][...]
    wide = NB * NOBS + MEMBERS
    eye = lax.broadcasted_iota(jnp.int32, (MEMBERS, MEMBERS), 0) == lax.broadcasted_iota(
        jnp.int32, (MEMBERS, MEMBERS), 1
    )
    state[:, NB * NOBS :] = jnp.where(eye, 1.0, 0.0)
    lanes = lax.broadcasted_iota(jnp.int32, (1, LANES), 1)
    diagonal = lax.broadcasted_iota(jnp.int32, (NOBS, LANES), 0) == lax.broadcasted_iota(
        jnp.int32, (NOBS, LANES), 1
    )
    scale = 1.0 / (MEMBERS - 1)
    for b in range(NB):
        here = slice(b * NOBS, (b + 1) * NOBS)
        live = lanes < counts_ref[b]
        priors = state[:, here]
        mean = jnp.sum(priors, 0, keepdims=True) * (1.0 / MEMBERS)
        pert = jnp.where(live, priors - mean, 0.0)
        innovation = jnp.where(live, obs_ref[0:1, here] - mean, 0.0)
        noise = jnp.where(live, obs_ref[1:2, here], 1.0)
        pert_t = pert.T
        cov = dot(pert_t, pert) * scale + jnp.where(diagonal, noise * noise, 0.0)
        crossed = dot(pert_t, state[:, (b + 1) * NOBS :])
        inv_l, inv_ld = eliminate(cov, noise)
        half = dot(inv_l, crossed)
        solved = dot(innovation, inv_l, 1, 1)
        if b < NB - 1:
            gain = (solved - dot(pert, inv_ld, 1, 1)) * scale
            state[:, (b + 1) * NOBS :] = state[:, (b + 1) * NOBS :] + dot(gain, half)
        else:
            gain = (solved - dot(pert[:members], inv_ld, 1, 1)) * scale
            out_ref[...] = state[:members, NB * NOBS : wide] + dot(gain, half)


def analysis(counts, obs, parts):
    members = MEMBERS // 8
    return pl.pallas_call(
        analysis_kernel,
        out_shape=jax.ShapeDtypeStruct((members, MEMBERS), jnp.float32),
        in_specs=[SMEM, VMEM] + [VMEM] * 8,
        out_specs=VMEM,
        scratch_shapes=[pltpu.VMEM((MEMBERS, NB * NOBS + MEMBERS), jnp.float32)],
        compiler_params=pltpu.CompilerParams(vmem_limit_bytes=32 << 20),
        name="analysis",
    )(counts, obs, *parts)


def update_kernel(mix_ref, *refs):
    parts, out_ref, state, sems = refs[:8], refs[8], refs[9], refs[10]
    members = out_ref.shape[0]
    copies = [
        pltpu.make_async_copy(parts[k], state.at[pl.ds(k * members, members)], sems.at[k]) for k in range(8)
    ]
    for copy in copies:
        copy.start()
    for copy in copies:
        copy.wait()
    out_ref[...] = dot(mix_ref[...], state[...])


def update(mix, parts):
    members, cells = parts[0].shape
    return pl.pallas_call(
        update_kernel,
        out_shape=jax.ShapeDtypeStruct((members, cells), jnp.float32),
        in_specs=[VMEM] + [HBM] * 8,
        out_specs=VMEM,
        scratch_shapes=[pltpu.VMEM((MEMBERS, cells), jnp.float32), pltpu.SemaphoreType.DMA((8,))],
        compiler_params=pltpu.CompilerParams(vmem_limit_bytes=32 << 20),
        name="update",
    )(mix, *parts)


def shift_x(k):
    return [(8 * x + r, 8 * ((x + k) % 4) + r) for x in range(4) for r in range(8)]


def shift_y(k):
    return [(8 * x + 2 * y + c, 8 * x + 2 * ((y + k) % 4) + c) for x in range(4) for y in range(4) for c in range(2)]


def shift_z(k):
    return [((z + k) % 8, z) for z in range(8)]


SWAP = [(i, i ^ 1) for i in range(32)]


def shards(ensemble, weights, blocks, owner_ids, counts, obs_values, obs_error):
    members = ensemble.shape[0]
    total = local_priors(owner_ids, ensemble, weights, blocks, obs_values, obs_error)
    up, down = [ensemble], [ensemble]

    def ring(ready):
        up.append(lax.ppermute(up[-1], "mem", shift_z(1)))
        down.append(lax.ppermute(down[-1], "mem", shift_z(7)))
        ready, up[-1], down[-1] = lax.optimization_barrier((ready, up[-1], down[-1]))
        return ready

    total = ring(total)
    for shift in (shift_x, shift_y):
        near, across, far = [lax.ppermute(total, "cell", shift(k)) for k in (1, 2, 3)]
        total = ring((total + across) + (near + far))
    middle = lax.ppermute(up[-1], "mem", shift_z(1))
    total = total + lax.ppermute(total, "cell", SWAP)
    own = total[:members]
    priors = [own] + [lax.ppermute(own, "mem", shift_z(k)) for k in range(1, 8)]
    mix = analysis(counts, total[members:], priors)
    return update(mix, up + [middle] + down[:0:-1])


def solution(mesh):
    return jax.shard_map(
        shards,
        mesh=mesh,
        in_specs=(P("mem", "cell"), P(), P(), P(), P(), P("cell", None), P("cell", None)),
        out_specs=P("mem", "cell"),
        check_vma=False,
    )
```

profile of v0, /device:TPU:2, one launch (start us, length us, event | category | flops | bytes accessed | tf_op | source)
XLA Modules:
  0.0 86.3 jit_solution(12374333530876872200)
XLA Ops:
  0.0 5.9 %collective-permute-start = (f32[32,2048]{1,0:T(8,128)}, f32[32,2048]{1,0:T(8,128)S(1)}, u32[]{:S(2)}, u32[]{:S(2)}) collective-permute-start(f32[32,2048]{1,0:T(8,128)} %refs_0_.1), channel_id=1, source_target_pairs={{1,0},{2,1},{3,2},{4,3},{5,4},{6,5},{7,6},{0,7},{9,8},{10,9},{11,1... | collective-permute-start | bytes 786440 | tf_op jit(solution)/shard_map/ppermute | solution.py:276
  5.9 5.4 %priors.1 = f32[40,512]{1,0:T(8,128)} custom-call(s32[4]{0:T(128)} %owners_ref.1, f32[32,2048]{1,0:T(8,128)} %refs_0_.1, f32[4,128,512]{2,1,0:T(8,128)} %weights_ref.1, s32[4,8,128]{2,1,0:T(8,128)} %bitcast.1, f32[4,128]{1,0:T(4,128)} %values_ref.1, f32[4,128]{1,0:T(4,128)} %error_ref.1), custom_call_target="tpu_custom_call" | custom-call | tf_op jit(solution)/shard_map/priors/pallas_call | solution.py:71
  11.3 0.5 collective-permute-done.refs_1_
  11.7 3.3 %collective-permute-done.1.refs_7_ = f32[32,2048]{1,0:T(8,128)S(1)} collective-permute-done((f32[32,2048]{1,0:T(8,128)}, f32[32,2048]{1,0:T(8,128)S(1)}, u32[]{:S(2)}, u32[]{:S(2)}) %collective-permute-start.1) | collective-permute-done | bytes 262176 | tf_op jit(solution)/shard_map/ppermute | solution.py:277
  15.0 0.5 collective-permute-start.4
  15.6 1.5 %collective-permute-start.3 = (f32[40,512]{1,0:T(8,128)}, f32[40,512]{1,0:T(8,128)S(1)}, u32[]{:S(2)}, u32[]{:S(2)}) collective-permute-start(f32[40,512]{1,0:T(8,128)} %priors.1), channel_id=1, source_target_pairs={{0,64},{8,72},{16,80},{24,88},{32,96},{40,104},{48,112},{56,120},{... | collective-permute-start | bytes 245768 | tf_op jit(solution)/shard_map/ppermute | solution.py:283
  17.1 3.3 %collective-permute-start.2 = (f32[40,512]{1,0:T(8,128)}, f32[40,512]{1,0:T(8,128)S(1)}, u32[]{:S(2)}, u32[]{:S(2)}) collective-permute-start(f32[40,512]{1,0:T(8,128)} %priors.1), channel_id=1, source_target_pairs={{0,128},{8,136},{16,144},{24,152},{32,160},{40,168},{48,176},{56,1... | collective-permute-start | bytes 245768 | tf_op jit(solution)/shard_map/ppermute | solution.py:283
  20.4 0.3 collective-permute-start.5
  20.7 1.7 %collective-permute-start.6 = (f32[32,2048]{1,0:T(8,128)S(1)}, f32[32,2048]{1,0:T(8,128)S(1)}, u32[]{:S(2)}, u32[]{:S(2)}) collective-permute-start(f32[32,2048]{1,0:T(8,128)S(1)} %collective-permute-done.1.refs_7_), channel_id=1, source_target_pairs={{7,0},{0,1},{1,2},{2,3},{3,4},{4,5},{5,6},{6,7},{15,8},{8,9},{9,10... | collective-permute-start | bytes 786440 | tf_op jit(solution)/shard_map/ppermute | solution.py:277
  22.4 0.8 collective-permute-done.2
  23.2 0.9 %add_add_fusion.1 = f32[40,512]{1,0:T(8,128)S(1)} fusion(f32[40,512]{1,0:T(8,128)S(1)} %collective-permute-done.3, f32[40,512]{1,0:T(8,128)S(1)} %collective-permute-done.4, f32[40,512]{1,0:T(8,128)} %priors.1, f32[40,512]{1,0:T(8,128)S(1)} %collective-permute-done.2), kind=kLoop, calls=%fused_computation.1 | loop fusion | flops 61440 | bytes 409600 | tf_op jit(solution)/shard_map/add | solution.py:284
  24.1 2.6 %collective-permute-done.5.refs_2_ = f32[32,2048]{1,0:T(8,128)S(1)} collective-permute-done((f32[32,2048]{1,0:T(8,128)S(1)}, f32[32,2048]{1,0:T(8,128)S(1)}, u32[]{:S(2)}, u32[]{:S(2)}) %collective-permute-start.5) | collective-permute-done | bytes 262176 | tf_op jit(solution)/shard_map/ppermute | solution.py:276
  26.8 1.5 %collective-permute-done.6.refs_6_ = f32[32,2048]{1,0:T(8,128)S(1)} collective-permute-done((f32[32,2048]{1,0:T(8,128)S(1)}, f32[32,2048]{1,0:T(8,128)S(1)}, u32[]{:S(2)}, u32[]{:S(2)}) %collective-permute-start.6) | collective-permute-done | bytes 262176 | tf_op jit(solution)/shard_map/ppermute | solution.py:277
  28.3 3.0 %collective-permute-start.9 = (f32[40,512]{1,0:T(8,128)S(1)}, f32[40,512]{1,0:T(8,128)S(1)}, u32[]{:S(2)}, u32[]{:S(2)}) collective-permute-start(f32[40,512]{1,0:T(8,128)S(1)} %add_add_fusion.1), channel_id=1, source_target_pairs={{0,48},{8,56},{16,0},{24,8},{32,16},{40,24},{48,32},{56,40},{64,11... | collective-permute-start | bytes 245768 | tf_op jit(solution)/shard_map/ppermute | solution.py:283
  31.3 2.2 %collective-permute-start.7 = (f32[40,512]{1,0:T(8,128)S(1)}, f32[40,512]{1,0:T(8,128)S(1)}, u32[]{:S(2)}, u32[]{:S(2)}) collective-permute-start(f32[40,512]{1,0:T(8,128)S(1)} %add_add_fusion.1), channel_id=1, source_target_pairs={{0,32},{8,40},{16,48},{24,56},{32,0},{40,8},{48,16},{56,24},{64,96... | collective-permute-start | bytes 245768 | tf_op jit(solution)/shard_map/ppermute | solution.py:283
  33.5 2.0 %collective-permute-start.11 = (f32[32,2048]{1,0:T(8,128)S(1)}, f32[32,2048]{1,0:T(8,128)S(1)}, u32[]{:S(2)}, u32[]{:S(2)}) collective-permute-start(f32[32,2048]{1,0:T(8,128)S(1)} %collective-permute-done.6.refs_6_), channel_id=1, source_target_pairs={{7,0},{0,1},{1,2},{2,3},{3,4},{4,5},{5,6},{6,7},{15,8},{8,9},{9,10... | collective-permute-start | bytes 786440 | tf_op jit(solution)/shard_map/ppermute | solution.py:277
  35.5 2.3 %collective-permute-done.8 = f32[40,512]{1,0:T(8,128)S(1)} collective-permute-done((f32[40,512]{1,0:T(8,128)S(1)}, f32[40,512]{1,0:T(8,128)S(1)}, u32[]{:S(2)}, u32[]{:S(2)}) %collective-permute-start.8) | collective-permute-done | bytes 81952 | tf_op jit(solution)/shard_map/ppermute | solution.py:283
  37.9 3.5 %collective-permute-done.10.refs_3_ = f32[32,2048]{1,0:T(8,128)S(1)} collective-permute-done((f32[32,2048]{1,0:T(8,128)S(1)}, f32[32,2048]{1,0:T(8,128)S(1)}, u32[]{:S(2)}, u32[]{:S(2)}) %collective-permute-start.10) | collective-permute-done | bytes 262176 | tf_op jit(solution)/shard_map/ppermute | solution.py:276
  41.3 0.6 collective-permute-start.20
  41.9 1.3 %collective-permute-done.12 = f32[40,512]{1,0:T(8,128)S(1)} collective-permute-done((f32[40,512]{1,0:T(8,128)S(1)}, f32[40,512]{1,0:T(8,128)S(1)}, u32[]{:S(2)}, u32[]{:S(2)}) %collective-permute-start.12) | collective-permute-done | bytes 81952 | tf_op jit(solution)/shard_map/ppermute | solution.py:286
  43.3 1.5 %collective-permute-start.19 = (f32[32,512]{1,0:T(8,128)S(1)}, f32[32,512]{1,0:T(8,128)S(1)}, u32[]{:S(2)}, u32[]{:S(2)}) collective-permute-start(f32[32,512]{1,0:T(8,128)S(1)} %slice.9.refs_0_), channel_id=1, source_target_pairs={{7,0},{0,1},{1,2},{2,3},{3,4},{4,5},{5,6},{6,7},{15,8},{8,9},{9,10... | collective-permute-start | bytes 196616 | tf_op jit(solution)/shard_map/ppermute | solution.py:288
  44.7 0.5 collective-permute-start.18
  45.3 1.6 %collective-permute-start.17 = (f32[32,512]{1,0:T(8,128)S(1)}, f32[32,512]{1,0:T(8,128)S(1)}, u32[]{:S(2)}, u32[]{:S(2)}) collective-permute-start(f32[32,512]{1,0:T(8,128)S(1)} %slice.9.refs_0_), channel_id=1, source_target_pairs={{5,0},{6,1},{7,2},{0,3},{1,4},{2,5},{3,6},{4,7},{13,8},{14,9},{15,... | collective-permute-start | bytes 196616 | tf_op jit(solution)/shard_map/ppermute | solution.py:288
  46.9 4.3 %collective-permute-start.16 = (f32[32,512]{1,0:T(8,128)S(1)}, f32[32,512]{1,0:T(8,128)S(1)}, u32[]{:S(2)}, u32[]{:S(2)}) collective-permute-start(f32[32,512]{1,0:T(8,128)S(1)} %slice.9.refs_0_), channel_id=1, source_target_pairs={{4,0},{5,1},{6,2},{7,3},{0,4},{1,5},{2,6},{3,7},{12,8},{13,9},{14,... | collective-permute-start | bytes 196616 | tf_op jit(solution)/shard_map/ppermute | solution.py:288
  51.3 0.9 %collective-permute-start.15 = (f32[32,512]{1,0:T(8,128)S(1)}, f32[32,512]{1,0:T(8,128)S(1)}, u32[]{:S(2)}, u32[]{:S(2)}) collective-permute-start(f32[32,512]{1,0:T(8,128)S(1)} %slice.9.refs_0_), channel_id=1, source_target_pairs={{3,0},{4,1},{5,2},{6,3},{7,4},{0,5},{1,6},{2,7},{11,8},{12,9},{13,... | collective-permute-start | bytes 196616 | tf_op jit(solution)/shard_map/ppermute | solution.py:288
  52.2 3.5 %collective-permute-done.18.refs_6_ = f32[32,512]{1,0:T(8,128)S(1)} collective-permute-done((f32[32,512]{1,0:T(8,128)S(1)}, f32[32,512]{1,0:T(8,128)S(1)}, u32[]{:S(2)}, u32[]{:S(2)}) %collective-permute-start.18) | collective-permute-done | bytes 65568 | tf_op jit(solution)/shard_map/ppermute | solution.py:288
  55.7 2.5 %collective-permute-start.13 = (f32[32,512]{1,0:T(8,128)S(1)}, f32[32,512]{1,0:T(8,128)S(1)}, u32[]{:S(2)}, u32[]{:S(2)}) collective-permute-start(f32[32,512]{1,0:T(8,128)S(1)} %slice.9.refs_0_), channel_id=1, source_target_pairs={{1,0},{2,1},{3,2},{4,3},{5,4},{6,5},{7,6},{0,7},{9,8},{10,9},{11,1... | collective-permute-start | bytes 196616 | tf_op jit(solution)/shard_map/ppermute | solution.py:288
  58.4 0.9 collective-permute-done.15.refs_3_
  59.3 4.1 %collective-permute-done.14.refs_2_ = f32[32,512]{1,0:T(8,128)S(1)} collective-permute-done((f32[32,512]{1,0:T(8,128)S(1)}, f32[32,512]{1,0:T(8,128)S(1)}, u32[]{:S(2)}, u32[]{:S(2)}) %collective-permute-start.14) | collective-permute-done | bytes 65568 | tf_op jit(solution)/shard_map/ppermute | solution.py:288
  63.4 0.3 collective-permute-done.13.refs_1_
  63.8 20.2 %analysis.1.mix_ref = f32[32,256]{1,0:T(8,128)S(1)} custom-call(s32[4]{0:T(128)S(1)} %copy-done.1, f32[8,512]{1,0:T(8,128)S(1)} %slice.8.obs_ref, f32[32,512]{1,0:T(8,128)S(1)} %slice.9.refs_0_, f32[32,512]{1,0:T(8,128)S(1)} %collective-permute-done.13.refs_1_, f32[32,512]{1,0:T(8,128)S(1)} %collective-permute-done.14.refs_2_, ...), custom_call_target="tpu_custom_call" | custom-call | tf_op jit(solution)/shard_map/analysis/pallas_call | solution.py:218
  83.9 2.1 %update.1 = f32[32,2048]{1,0:T(8,128)} custom-call(f32[32,256]{1,0:T(8,128)S(1)} %analysis.1.mix_ref, f32[32,2048]{1,0:T(8,128)S(1)} %copy-done, f32[32,2048]{1,0:T(8,128)S(1)} %collective-permute-done.refs_1_, f32[32,2048]{1,0:T(8,128)S(1)} %collective-permute-done.5.refs_2_, f32[32,2048]{1,0:T(8,128)S(1)} %collective-permute-done.10.refs_3_, ...), custom_call_target="tpu_custom_call" | custom-call | tf_op jit(solution)/shard_map/update/pallas_call | solution.py:244
  (22 shorter events, 0.3 us)
Async XLA Ops:
  0.0 11.7 %collective-permute-start = (f32[32,2048]{1,0:T(8,128)}, f32[32,2048]{1,0:T(8,128)S(1)}, u32[]{:S(2)}, u32[]{:S(2)}) collective-permute-start(f32[32,2048]{1,0:T(8,128)} %refs_0_.1), channel_id=1, source_target_pairs={{1,0},{2,1},{3,2},{4,3},{5,4},{6,5},{7,6},{0,7},{9,8},{10,9},{11,1... | collective-permute-start | bytes 786440 | tf_op jit(solution)/shard_map/ppermute | solution.py:276
  5.9 9.2 %collective-permute-start.1 = (f32[32,2048]{1,0:T(8,128)}, f32[32,2048]{1,0:T(8,128)S(1)}, u32[]{:S(2)}, u32[]{:S(2)}) collective-permute-start(f32[32,2048]{1,0:T(8,128)} %refs_0_.1), channel_id=1, source_target_pairs={{7,0},{0,1},{1,2},{2,3},{3,4},{4,5},{5,6},{6,7},{15,8},{8,9},{9,10... | collective-permute-start | bytes 786440 | tf_op jit(solution)/shard_map/ppermute | solution.py:277
  15.0 7.4 %collective-permute-start.4 = (f32[40,512]{1,0:T(8,128)}, f32[40,512]{1,0:T(8,128)S(1)}, u32[]{:S(2)}, u32[]{:S(2)}) collective-permute-start(f32[40,512]{1,0:T(8,128)} %priors.1), channel_id=1, source_target_pairs={{0,192},{8,200},{16,208},{24,216},{32,224},{40,232},{48,240},{56,2... | collective-permute-start | bytes 245768 | tf_op jit(solution)/shard_map/ppermute | solution.py:283
  15.6 6.9 %collective-permute-start.3 = (f32[40,512]{1,0:T(8,128)}, f32[40,512]{1,0:T(8,128)S(1)}, u32[]{:S(2)}, u32[]{:S(2)}) collective-permute-start(f32[40,512]{1,0:T(8,128)} %priors.1), channel_id=1, source_target_pairs={{0,64},{8,72},{16,80},{24,88},{32,96},{40,104},{48,112},{56,120},{... | collective-permute-start | bytes 245768 | tf_op jit(solution)/shard_map/ppermute | solution.py:283
  17.1 6.2 %collective-permute-start.2 = (f32[40,512]{1,0:T(8,128)}, f32[40,512]{1,0:T(8,128)S(1)}, u32[]{:S(2)}, u32[]{:S(2)}) collective-permute-start(f32[40,512]{1,0:T(8,128)} %priors.1), channel_id=1, source_target_pairs={{0,128},{8,136},{16,144},{24,152},{32,160},{40,168},{48,176},{56,1... | collective-permute-start | bytes 245768 | tf_op jit(solution)/shard_map/ppermute | solution.py:283
  20.4 6.4 %collective-permute-start.5 = (f32[32,2048]{1,0:T(8,128)S(1)}, f32[32,2048]{1,0:T(8,128)S(1)}, u32[]{:S(2)}, u32[]{:S(2)}) collective-permute-start(f32[32,2048]{1,0:T(8,128)S(1)} %collective-permute-done.refs_1_), channel_id=1, source_target_pairs={{1,0},{2,1},{3,2},{4,3},{5,4},{6,5},{7,6},{0,7},{9,8},{10,9},{11,1... | collective-permute-start | bytes 786440 | tf_op jit(solution)/shard_map/ppermute | solution.py:276
  20.7 7.6 %collective-permute-start.6 = (f32[32,2048]{1,0:T(8,128)S(1)}, f32[32,2048]{1,0:T(8,128)S(1)}, u32[]{:S(2)}, u32[]{:S(2)}) collective-permute-start(f32[32,2048]{1,0:T(8,128)S(1)} %collective-permute-done.1.refs_7_), channel_id=1, source_target_pairs={{7,0},{0,1},{1,2},{2,3},{3,4},{4,5},{5,6},{6,7},{15,8},{8,9},{9,10... | collective-permute-start | bytes 786440 | tf_op jit(solution)/shard_map/ppermute | solution.py:277
  28.3 7.3 %collective-permute-start.9 = (f32[40,512]{1,0:T(8,128)S(1)}, f32[40,512]{1,0:T(8,128)S(1)}, u32[]{:S(2)}, u32[]{:S(2)}) collective-permute-start(f32[40,512]{1,0:T(8,128)S(1)} %add_add_fusion.1), channel_id=1, source_target_pairs={{0,48},{8,56},{16,0},{24,8},{32,16},{40,24},{48,32},{56,40},{64,11... | collective-permute-start | bytes 245768 | tf_op jit(solution)/shard_map/ppermute | solution.py:283
  31.3 6.5 %collective-permute-start.8 = (f32[40,512]{1,0:T(8,128)S(1)}, f32[40,512]{1,0:T(8,128)S(1)}, u32[]{:S(2)}, u32[]{:S(2)}) collective-permute-start(f32[40,512]{1,0:T(8,128)S(1)} %add_add_fusion.1), channel_id=1, source_target_pairs={{0,16},{8,24},{16,32},{24,40},{32,48},{40,56},{48,0},{56,8},{64,80... | collective-permute-start | bytes 245768 | tf_op jit(solution)/shard_map/ppermute | solution.py:283
  31.3 6.5 %collective-permute-start.7 = (f32[40,512]{1,0:T(8,128)S(1)}, f32[40,512]{1,0:T(8,128)S(1)}, u32[]{:S(2)}, u32[]{:S(2)}) collective-permute-start(f32[40,512]{1,0:T(8,128)S(1)} %add_add_fusion.1), channel_id=1, source_target_pairs={{0,32},{8,40},{16,48},{24,56},{32,0},{40,8},{48,16},{56,24},{64,96... | collective-permute-start | bytes 245768 | tf_op jit(solution)/shard_map/ppermute | solution.py:283
  33.5 7.8 %collective-permute-start.10 = (f32[32,2048]{1,0:T(8,128)S(1)}, f32[32,2048]{1,0:T(8,128)S(1)}, u32[]{:S(2)}, u32[]{:S(2)}) collective-permute-start(f32[32,2048]{1,0:T(8,128)S(1)} %collective-permute-done.5.refs_2_), channel_id=1, source_target_pairs={{1,0},{2,1},{3,2},{4,3},{5,4},{6,5},{7,6},{0,7},{9,8},{10,9},{11,1... | collective-permute-start | bytes 786440 | tf_op jit(solution)/shard_map/ppermute | solution.py:276
  33.5 7.8 %collective-permute-start.11 = (f32[32,2048]{1,0:T(8,128)S(1)}, f32[32,2048]{1,0:T(8,128)S(1)}, u32[]{:S(2)}, u32[]{:S(2)}) collective-permute-start(f32[32,2048]{1,0:T(8,128)S(1)} %collective-permute-done.6.refs_6_), channel_id=1, source_target_pairs={{7,0},{0,1},{1,2},{2,3},{3,4},{4,5},{5,6},{6,7},{15,8},{8,9},{9,10... | collective-permute-start | bytes 786440 | tf_op jit(solution)/shard_map/ppermute | solution.py:277
  41.3 42.6 %collective-permute-start.20 = (f32[32,2048]{1,0:T(8,128)S(1)}, f32[32,2048]{1,0:T(8,128)S(1)}, u32[]{:S(2)}, u32[]{:S(2)}) collective-permute-start(f32[32,2048]{1,0:T(8,128)S(1)} %collective-permute-done.10.refs_3_), channel_id=1, source_target_pairs={{1,0},{2,1},{3,2},{4,3},{5,4},{6,5},{7,6},{0,7},{9,8},{10,9},{11,1... | collective-permute-start | bytes 786440 | tf_op jit(solution)/shard_map/ppermute | solution.py:285
  41.9 1.3 %collective-permute-start.12 = (f32[40,512]{1,0:T(8,128)S(1)}, f32[40,512]{1,0:T(8,128)S(1)}, u32[]{:S(2)}, u32[]{:S(2)}) collective-permute-start(f32[40,512]{1,0:T(8,128)S(1)} %add_add_fusion), channel_id=1, source_target_pairs={{0,8},{8,0},{16,24},{24,16},{32,40},{40,32},{48,56},{56,48},{64,72... | collective-permute-start | bytes 245768 | tf_op jit(solution)/shard_map/ppermute | solution.py:286
  43.2 20.5 %copy-start.1 = (s32[4]{0:T(128)S(1)}, s32[4]{0:T(128)}, u32[]{:S(2)}) copy-start(s32[4]{0:T(128)} %counts_ref.1) | copy-start | bytes 52
  43.3 8.0 %collective-permute-start.19 = (f32[32,512]{1,0:T(8,128)S(1)}, f32[32,512]{1,0:T(8,128)S(1)}, u32[]{:S(2)}, u32[]{:S(2)}) collective-permute-start(f32[32,512]{1,0:T(8,128)S(1)} %slice.9.refs_0_), channel_id=1, source_target_pairs={{7,0},{0,1},{1,2},{2,3},{3,4},{4,5},{5,6},{6,7},{15,8},{8,9},{9,10... | collective-permute-start | bytes 196616 | tf_op jit(solution)/shard_map/ppermute | solution.py:288
  44.7 11.0 %collective-permute-start.18 = (f32[32,512]{1,0:T(8,128)S(1)}, f32[32,512]{1,0:T(8,128)S(1)}, u32[]{:S(2)}, u32[]{:S(2)}) collective-permute-start(f32[32,512]{1,0:T(8,128)S(1)} %slice.9.refs_0_), channel_id=1, source_target_pairs={{6,0},{7,1},{0,2},{1,3},{2,4},{3,5},{4,6},{5,7},{14,8},{15,9},{8,1... | collective-permute-start | bytes 196616 | tf_op jit(solution)/shard_map/ppermute | solution.py:288
  45.3 10.5 %collective-permute-start.17 = (f32[32,512]{1,0:T(8,128)S(1)}, f32[32,512]{1,0:T(8,128)S(1)}, u32[]{:S(2)}, u32[]{:S(2)}) collective-permute-start(f32[32,512]{1,0:T(8,128)S(1)} %slice.9.refs_0_), channel_id=1, source_target_pairs={{5,0},{6,1},{7,2},{0,3},{1,4},{2,5},{3,6},{4,7},{13,8},{14,9},{15,... | collective-permute-start | bytes 196616 | tf_op jit(solution)/shard_map/ppermute | solution.py:288
  46.9 11.5 %collective-permute-start.16 = (f32[32,512]{1,0:T(8,128)S(1)}, f32[32,512]{1,0:T(8,128)S(1)}, u32[]{:S(2)}, u32[]{:S(2)}) collective-permute-start(f32[32,512]{1,0:T(8,128)S(1)} %slice.9.refs_0_), channel_id=1, source_target_pairs={{4,0},{5,1},{6,2},{7,3},{0,4},{1,5},{2,6},{3,7},{12,8},{13,9},{14,... | collective-permute-start | bytes 196616 | tf_op jit(solution)/shard_map/ppermute | solution.py:288
  51.3 8.0 %collective-permute-start.15 = (f32[32,512]{1,0:T(8,128)S(1)}, f32[32,512]{1,0:T(8,128)S(1)}, u32[]{:S(2)}, u32[]{:S(2)}) collective-permute-start(f32[32,512]{1,0:T(8,128)S(1)} %slice.9.refs_0_), channel_id=1, source_target_pairs={{3,0},{4,1},{5,2},{6,3},{7,4},{0,5},{1,6},{2,7},{11,8},{12,9},{13,... | collective-permute-start | bytes 196616 | tf_op jit(solution)/shard_map/ppermute | solution.py:288
  55.7 7.7 %collective-permute-start.14 = (f32[32,512]{1,0:T(8,128)S(1)}, f32[32,512]{1,0:T(8,128)S(1)}, u32[]{:S(2)}, u32[]{:S(2)}) collective-permute-start(f32[32,512]{1,0:T(8,128)S(1)} %slice.9.refs_0_), channel_id=1, source_target_pairs={{2,0},{3,1},{4,2},{5,3},{6,4},{7,5},{0,6},{1,7},{10,8},{11,9},{12,... | collective-permute-start | bytes 196616 | tf_op jit(solution)/shard_map/ppermute | solution.py:288
  55.7 8.0 %collective-permute-start.13 = (f32[32,512]{1,0:T(8,128)S(1)}, f32[32,512]{1,0:T(8,128)S(1)}, u32[]{:S(2)}, u32[]{:S(2)}) collective-permute-start(f32[32,512]{1,0:T(8,128)S(1)} %slice.9.refs_0_), channel_id=1, source_target_pairs={{1,0},{2,1},{3,2},{4,3},{5,4},{6,5},{7,6},{0,7},{9,8},{10,9},{11,1... | collective-permute-start | bytes 196616 | tf_op jit(solution)/shard_map/ppermute | solution.py:288
  58.2 25.7 %copy-start = (f32[32,2048]{1,0:T(8,128)S(1)}, f32[32,2048]{1,0:T(8,128)}, u32[]{:S(2)}) copy-start(f32[32,2048]{1,0:T(8,128)} %refs_0_.1) | copy-start | bytes 786436
where the time goes:
time: 86.7 us; the launch traced here: 86.3 us
  starting transfers between devices  32.5 us (37%)
  Pallas kernels  27.7 us (32%)
  waiting for transfers between devices  24.8 us (29%)
  other arithmetic  0.95 us (1%)
    pallas_call x1, Pallas kernels, analysis(): pl.pallas_call(analysis_kernel, out_shape=jax.ShapeDtypeStruct((members,...  20.2 us
    ppermute x7, starting transfers between devices, shards(): priors = [own] + [lax.ppermute(own, 'mem', shift_z(k)) for k in range(1, 8)]  11.4 us
    ppermute x6, starting transfers between devices, shards(): lax.ppermute(total, 'cell', shift(k))  10.6 us
    ppermute x7, waiting for transfers between devices, shards(): priors = [own] + [lax.ppermute(own, 'mem', shift_z(k)) for k in range(1, 8)]  9.09 us
    ppermute x3, waiting for transfers between devices, ring(): up.append(lax.ppermute(up[-1], 'mem', shift_z(1)))  6.55 us
    ppermute x3, starting transfers between devices, ring(): up.append(lax.ppermute(up[-1], 'mem', shift_z(1)))  6.14 us
    pallas_call x1, Pallas kernels, local_priors(): pl.pallas_call(priors_kernel, out_shape=jax.ShapeDtypeStruct((members + S...  5.42 us
    ppermute x3, waiting for transfers between devices, ring(): down.append(lax.ppermute(down[-1], 'mem', shift_z(7)))  4.8 us
  transfers between devices with their start and end apart: 21, of which 13 were waited for; matrix products, arithmetic and copies ran while one was open for 1% of the time, Pallas kernels for 30%

commit v1 on v0

--- a/solution.py
+++ b/solution.py
@@ -176,54 +176,72 @@
     return jnp.concatenate(z, 0), jnp.concatenate(y, 0)
 
 
-def analysis_kernel(counts_ref, obs_ref, *refs):
-    members = MEMBERS // 8
-    parts, out_ref, state = refs[:8], refs[8], refs[9]
-    for k in range(8):
-        state[k * members : (k + 1) * members, : NB * NOBS] = parts[k][...]
-    wide = NB * NOBS + MEMBERS
-    eye = lax.broadcasted_iota(jnp.int32, (MEMBERS, MEMBERS), 0) == lax.broadcasted_iota(
-        jnp.int32, (MEMBERS, MEMBERS), 1
-    )
-    state[:, NB * NOBS :] = jnp.where(eye, 1.0, 0.0)
+def analyse(batches, counts_ref, obs_ref, state, out_ref):
     lanes = lax.broadcasted_iota(jnp.int32, (1, LANES), 1)
     diagonal = lax.broadcasted_iota(jnp.int32, (NOBS, LANES), 0) == lax.broadcasted_iota(
         jnp.int32, (NOBS, LANES), 1
     )
     scale = 1.0 / (MEMBERS - 1)
-    for b in range(NB):
-        here = slice(b * NOBS, (b + 1) * NOBS)
+    for at, b in enumerate(batches):
+        here, rest = slice(at * NOBS, (at + 1) * NOBS), slice((at + 1) * NOBS, None)
         live = lanes < counts_ref[b]
         priors = state[:, here]
         mean = jnp.sum(priors, 0, keepdims=True) * (1.0 / MEMBERS)
         pert = jnp.where(live, priors - mean, 0.0)
-        innovation = jnp.where(live, obs_ref[0:1, here] - mean, 0.0)
-        noise = jnp.where(live, obs_ref[1:2, here], 1.0)
+        innovation = jnp.where(live, obs_ref[0:1, b * NOBS : (b + 1) * NOBS] - mean, 0.0)
+        noise = jnp.where(live, obs_ref[1:2, b * NOBS : (b + 1) * NOBS], 1.0)
         pert_t = pert.T
         cov = dot(pert_t, pert) * scale + jnp.where(diagonal, noise * noise, 0.0)
-        crossed = dot(pert_t, state[:, (b + 1) * NOBS :])
+        crossed = dot(pert_t, state[:, rest])
         inv_l, inv_ld = eliminate(cov, noise)
         half = dot(inv_l, crossed)
         solved = dot(innovation, inv_l, 1, 1)
         if b < NB - 1:
             gain = (solved - dot(pert, inv_ld, 1, 1)) * scale
-            state[:, (b + 1) * NOBS :] = state[:, (b + 1) * NOBS :] + dot(gain, half)
+            changed = state[:, rest] + dot(gain, half)
+            if at < len(batches) - 1:
+                state[:, rest] = changed
+            else:
+                out_ref[...] = changed
         else:
+            members = out_ref.shape[0]
             gain = (solved - dot(pert[:members], inv_ld, 1, 1)) * scale
-            out_ref[...] = state[:members, NB * NOBS : wide] + dot(gain, half)
-
-
-def analysis(counts, obs, parts):
+            out_ref[...] = state[:members, rest] + dot(gain, half)
+
+
+EARLY, LATE = range(NB // 2), range(NB // 2, NB)
+
+
+def early_kernel(counts_ref, obs_ref, *refs):
+    parts, out_ref, state = refs[:8], refs[8], refs[9]
     members = MEMBERS // 8
+    for k in range(8):
+        state[k * members : (k + 1) * members, : NB * NOBS] = parts[k][...]
+    eye = lax.broadcasted_iota(jnp.int32, (MEMBERS, MEMBERS), 0) == lax.broadcasted_iota(
+        jnp.int32, (MEMBERS, MEMBERS), 1
+    )
+    state[:, NB * NOBS :] = jnp.where(eye, 1.0, 0.0)
+    analyse(EARLY, counts_ref, obs_ref, state, out_ref)
+
+
+def late_kernel(counts_ref, obs_ref, state_ref, out_ref, state):
+    state[...] = state_ref[...]
+    analyse(LATE, counts_ref, obs_ref, state, out_ref)
+
+
+def analysis(counts, obs, arrays, batches):
+    early = batches is EARLY
+    wide = NB * NOBS + MEMBERS - batches[0] * NOBS
+    shape = (MEMBERS, wide - len(batches) * NOBS) if early else (MEMBERS // 8, MEMBERS)
     return pl.pallas_call(
-        analysis_kernel,
-        out_shape=jax.ShapeDtypeStruct((members, MEMBERS), jnp.float32),
-        in_specs=[SMEM, VMEM] + [VMEM] * 8,
+        early_kernel if early else late_kernel,
+        out_shape=jax.ShapeDtypeStruct(shape, jnp.float32),
+        in_specs=[SMEM] + [VMEM] * (1 + len(arrays)),
         out_specs=VMEM,
-        scratch_shapes=[pltpu.VMEM((MEMBERS, NB * NOBS + MEMBERS), jnp.float32)],
+        scratch_shapes=[pltpu.VMEM((MEMBERS, wide), jnp.float32)],
         compiler_params=pltpu.CompilerParams(vmem_limit_bytes=32 << 20),
-        name="analysis",
-    )(counts, obs, *parts)
+        name="early" if early else "late",
+    )(counts, obs, *arrays)
 
 
 def update_kernel(mix_ref, *refs):
@@ -272,21 +290,31 @@
     total = local_priors(owner_ids, ensemble, weights, blocks, obs_values, obs_error)
     up, down = [ensemble], [ensemble]
 
-    def ring(ready):
+    def ring(up, down):
         up.append(lax.ppermute(up[-1], "mem", shift_z(1)))
         down.append(lax.ppermute(down[-1], "mem", shift_z(7)))
+
+    def tie(ready):
         ready, up[-1], down[-1] = lax.optimization_barrier((ready, up[-1], down[-1]))
         return ready
 
-    total = ring(total)
+    ring(up, down)
+    total = tie(total)
+    ring(up, down)
     for shift in (shift_x, shift_y):
         near, across, far = [lax.ppermute(total, "cell", shift(k)) for k in (1, 2, 3)]
-        total = ring((total + across) + (near + far))
+        total = (total + across) + (near + far)
+    total = tie(total)
+    total = total + lax.ppermute(total, "cell", SWAP)
+    right, left = [total[:members]], [total[:members]]
+    for _ in range(3):
+        ring(right, left)
+    far = lax.ppermute(right[-1], "mem", shift_z(1))
+    priors = tie(right + [far] + left[:0:-1])
+    ring(up, down)
+    state = tie(analysis(counts, total[members:], priors, EARLY))
     middle = lax.ppermute(up[-1], "mem", shift_z(1))
-    total = total + lax.ppermute(total, "cell", SWAP)
-    own = total[:members]
-    priors = [own] + [lax.ppermute(own, "mem", shift_z(k)) for k in range(1, 8)]
-    mix = analysis(counts, total[members:], priors)
+    mix = analysis(counts, total[members:], [state], LATE)
     return update(mix, up + [middle] + down[:0:-1])
 
 

time: 86.7 us -> 89 us (1.027); the launches traced: 86.3 us -> 87.2 us
  starting transfers between devices: 32.5 us -> 35.9 us
  waiting for transfers between devices: 24.8 us -> 22 us
    ppermute x7 -> x1, starting transfers between devices: 11.4 us -> 3.57 us  [shards(): far = lax.ppermute(right[-1], 'mem', shift_z(1))]
    ppermute x3 -> x6, starting transfers between devices: 6.14 us -> 13.8 us  [ring(): up.append(lax.ppermute(up[-1], 'mem', shift_z(1)))]
    ppermute x7 -> x1, waiting for transfers between devices: 9.09 us -> 1.81 us  [shards(): far = lax.ppermute(right[-1], 'mem', shift_z(1))]
    ppermute x1, starting transfers between devices: 0.62 us -> 3.56 us  [shards(): middle = lax.ppermute(up[-1], 'mem', shift_z(1))]
    ppermute x3 -> x6, waiting for transfers between devices: 6.55 us -> 8.75 us  [ring(): up.append(lax.ppermute(up[-1], 'mem', shift_z(1)))]
    ppermute x6, waiting for transfers between devices: 3.09 us -> 5.12 us  [shards(): lax.ppermute(total, 'cell', shift(k))]
    ppermute x3 -> x6, starting transfers between devices: 3.77 us -> 4.31 us  [ring(): down.append(lax.ppermute(down[-1], 'mem', shift_z(7)))]
    ppermute x3 -> x6, waiting for transfers between devices: 4.8 us -> 5.1 us  [ring(): down.append(lax.ppermute(down[-1], 'mem', shift_z(7)))]
  transfers between devices with their start and end apart: 21 -> 21, of which waited for: 13 -> 15; matrix products, arithmetic and copies ran while one was open for 1% -> 0% of each run, Pallas kernels for 30% -> 30%
where the time goes in v1:
time: 89 us; the launch traced here: 87.2 us
  starting transfers between devices  35.9 us (40%)
  Pallas kernels  28 us (31%)
  waiting for transfers between devices  22 us (25%)
  other arithmetic  0.95 us (1%)
    pallas_call x2, Pallas kernels, analysis(): pl.pallas_call(early_kernel if early else late_kernel, out_shape=jax.Shap...  20.4 us
    ppermute x6, starting transfers between devices, ring(): up.append(lax.ppermute(up[-1], 'mem', shift_z(1)))  13.8 us
    ppermute x6, starting transfers between devices, shards(): lax.ppermute(total, 'cell', shift(k))  10.7 us
    ppermute x6, waiting for transfers between devices, ring(): up.append(lax.ppermute(up[-1], 'mem', shift_z(1)))  8.75 us
    pallas_call x1, Pallas kernels, local_priors(): pl.pallas_call(priors_kernel, out_shape=jax.ShapeDtypeStruct((members + S...  5.42 us
    ppermute x6, waiting for transfers between devices, shards(): lax.ppermute(total, 'cell', shift(k))  5.12 us
    ppermute x6, waiting for transfers between devices, ring(): down.append(lax.ppermute(down[-1], 'mem', shift_z(7)))  5.1 us
    ppermute x6, starting transfers between devices, ring(): down.append(lax.ppermute(down[-1], 'mem', shift_z(7)))  4.31 us
  transfers between devices with their start and end apart: 21, of which 15 were waited for; matrix products, arithmetic and copies ran while one was open for 0% of the time, Pallas kernels for 30%

profile of v1, /device:TPU:2, one launch (start us, length us, event | category | flops | bytes accessed | tf_op | source)
XLA Modules:
  0.0 87.2 jit_solution(18092309591393461928)
XLA Ops:
  0.0 5.9 %collective-permute-start = (f32[32,2048]{1,0:T(8,128)}, f32[32,2048]{1,0:T(8,128)S(1)}, u32[]{:S(2)}, u32[]{:S(2)}) collective-permute-start(f32[32,2048]{1,0:T(8,128)} %refs_0_.1), channel_id=1, source_target_pairs={{1,0},{2,1},{3,2},{4,3},{5,4},{6,5},{7,6},{0,7},{9,8},{10,9},{11,1... | collective-permute-start | bytes 786440 | tf_op jit(solution)/shard_map/ppermute | solution.py:294
  5.9 5.4 %priors.1 = f32[40,512]{1,0:T(8,128)} custom-call(s32[4]{0:T(128)} %owners_ref.1, f32[32,2048]{1,0:T(8,128)} %refs_0_.1, f32[4,128,512]{2,1,0:T(8,128)} %weights_ref.1, s32[4,8,128]{2,1,0:T(8,128)} %bitcast.1, f32[4,128]{1,0:T(4,128)} %values_ref.1, f32[4,128]{1,0:T(4,128)} %error_ref.1), custom_call_target="tpu_custom_call" | custom-call | tf_op jit(solution)/shard_map/priors/pallas_call | solution.py:71
  11.3 0.5 collective-permute-done.refs_1_
  11.7 3.3 %collective-permute-done.1.refs_7_ = f32[32,2048]{1,0:T(8,128)S(1)} collective-permute-done((f32[32,2048]{1,0:T(8,128)}, f32[32,2048]{1,0:T(8,128)S(1)}, u32[]{:S(2)}, u32[]{:S(2)}) %collective-permute-start.1) | collective-permute-done | bytes 262176 | tf_op jit(solution)/shard_map/ppermute | solution.py:295
  15.0 0.5 collective-permute-start.4
  15.6 1.5 %collective-permute-start.3 = (f32[40,512]{1,0:T(8,128)}, f32[40,512]{1,0:T(8,128)S(1)}, u32[]{:S(2)}, u32[]{:S(2)}) collective-permute-start(f32[40,512]{1,0:T(8,128)} %priors.1), channel_id=1, source_target_pairs={{0,64},{8,72},{16,80},{24,88},{32,96},{40,104},{48,112},{56,120},{... | collective-permute-start | bytes 245768 | tf_op jit(solution)/shard_map/ppermute | solution.py:305
  17.1 3.3 %collective-permute-start.2 = (f32[40,512]{1,0:T(8,128)}, f32[40,512]{1,0:T(8,128)S(1)}, u32[]{:S(2)}, u32[]{:S(2)}) collective-permute-start(f32[40,512]{1,0:T(8,128)} %priors.1), channel_id=1, source_target_pairs={{0,128},{8,136},{16,144},{24,152},{32,160},{40,168},{48,176},{56,1... | collective-permute-start | bytes 245768 | tf_op jit(solution)/shard_map/ppermute | solution.py:305
  20.4 0.8 collective-permute-done.3
  21.2 2.0 %collective-permute-done.2 = f32[40,512]{1,0:T(8,128)S(1)} collective-permute-done((f32[40,512]{1,0:T(8,128)}, f32[40,512]{1,0:T(8,128)S(1)}, u32[]{:S(2)}, u32[]{:S(2)}) %collective-permute-start.2) | collective-permute-done | bytes 81952 | tf_op jit(solution)/shard_map/ppermute | solution.py:305
  23.2 0.9 %add_add_fusion.1 = f32[40,512]{1,0:T(8,128)S(1)} fusion(f32[40,512]{1,0:T(8,128)S(1)} %collective-permute-done.3, f32[40,512]{1,0:T(8,128)S(1)} %collective-permute-done.4, f32[40,512]{1,0:T(8,128)} %priors.1, f32[40,512]{1,0:T(8,128)S(1)} %collective-permute-done.2), kind=kLoop, calls=%fused_computation.1 | loop fusion | flops 61440 | bytes 409600 | tf_op jit(solution)/shard_map/add | solution.py:306
  24.1 3.1 %collective-permute-start.7 = (f32[40,512]{1,0:T(8,128)S(1)}, f32[40,512]{1,0:T(8,128)S(1)}, u32[]{:S(2)}, u32[]{:S(2)}) collective-permute-start(f32[40,512]{1,0:T(8,128)S(1)} %add_add_fusion.1), channel_id=1, source_target_pairs={{0,48},{8,56},{16,0},{24,8},{32,16},{40,24},{48,32},{56,40},{64,11... | collective-permute-start | bytes 245768 | tf_op jit(solution)/shard_map/ppermute | solution.py:305
  27.2 2.2 %collective-permute-start.5 = (f32[40,512]{1,0:T(8,128)S(1)}, f32[40,512]{1,0:T(8,128)S(1)}, u32[]{:S(2)}, u32[]{:S(2)}) collective-permute-start(f32[40,512]{1,0:T(8,128)S(1)} %add_add_fusion.1), channel_id=1, source_target_pairs={{0,32},{8,40},{16,48},{24,56},{32,0},{40,8},{48,16},{56,24},{64,96... | collective-permute-start | bytes 245768 | tf_op jit(solution)/shard_map/ppermute | solution.py:305
  29.4 0.3 collective-permute-start.8
  29.7 1.7 %collective-permute-start.9 = (f32[32,2048]{1,0:T(8,128)S(1)}, f32[32,2048]{1,0:T(8,128)S(1)}, u32[]{:S(2)}, u32[]{:S(2)}) collective-permute-start(f32[32,2048]{1,0:T(8,128)S(1)} %collective-permute-done.1.refs_7_), channel_id=1, source_target_pairs={{7,0},{0,1},{1,2},{2,3},{3,4},{4,5},{5,6},{6,7},{15,8},{8,9},{9,10... | collective-permute-start | bytes 786440 | tf_op jit(solution)/shard_map/ppermute | solution.py:295
  31.5 2.3 %collective-permute-done.6 = f32[40,512]{1,0:T(8,128)S(1)} collective-permute-done((f32[40,512]{1,0:T(8,128)S(1)}, f32[40,512]{1,0:T(8,128)S(1)}, u32[]{:S(2)}, u32[]{:S(2)}) %collective-permute-start.6) | collective-permute-done | bytes 81952 | tf_op jit(solution)/shard_map/ppermute | solution.py:305
  33.8 2.0 %collective-permute-done.8.refs_2_ = f32[32,2048]{1,0:T(8,128)S(1)} collective-permute-done((f32[32,2048]{1,0:T(8,128)S(1)}, f32[32,2048]{1,0:T(8,128)S(1)}, u32[]{:S(2)}, u32[]{:S(2)}) %collective-permute-start.8) | collective-permute-done | bytes 262176 | tf_op jit(solution)/shard_map/ppermute | solution.py:294
  35.8 1.5 %collective-permute-done.9.refs_6_ = f32[32,2048]{1,0:T(8,128)S(1)} collective-permute-done((f32[32,2048]{1,0:T(8,128)S(1)}, f32[32,2048]{1,0:T(8,128)S(1)}, u32[]{:S(2)}, u32[]{:S(2)}) %collective-permute-start.9) | collective-permute-done | bytes 262176 | tf_op jit(solution)/shard_map/ppermute | solution.py:295
  37.3 1.3 %collective-permute-done.10 = f32[40,512]{1,0:T(8,128)S(1)} collective-permute-done((f32[40,512]{1,0:T(8,128)S(1)}, f32[40,512]{1,0:T(8,128)S(1)}, u32[]{:S(2)}, u32[]{:S(2)}) %collective-permute-start.10) | collective-permute-done | bytes 81952 | tf_op jit(solution)/shard_map/ppermute | solution.py:308
  38.7 2.0 %collective-permute-start.15 = (f32[32,512]{1,0:T(8,128)S(1)}, f32[32,512]{1,0:T(8,128)S(1)}, u32[]{:S(2)}, u32[]{:S(2)}) collective-permute-start(f32[32,512]{1,0:T(8,128)S(1)} %slice.11.refs_0_), channel_id=1, source_target_pairs={{7,0},{0,1},{1,2},{2,3},{3,4},{4,5},{5,6},{6,7},{15,8},{8,9},{9,10... | collective-permute-start | bytes 196616 | tf_op jit(solution)/shard_map/ppermute | solution.py:295
  40.7 2.2 %collective-permute-done.11.refs_1_ = f32[32,512]{1,0:T(8,128)S(1)} collective-permute-done((f32[32,512]{1,0:T(8,128)S(1)}, f32[32,512]{1,0:T(8,128)S(1)}, u32[]{:S(2)}, u32[]{:S(2)}) %collective-permute-start.11) | collective-permute-done | bytes 65568 | tf_op jit(solution)/shard_map/ppermute | solution.py:294
  43.0 1.4 %collective-permute-start.12 = (f32[32,512]{1,0:T(8,128)S(1)}, f32[32,512]{1,0:T(8,128)S(1)}, u32[]{:S(2)}, u32[]{:S(2)}) collective-permute-start(f32[32,512]{1,0:T(8,128)S(1)} %collective-permute-done.11.refs_1_), channel_id=1, source_target_pairs={{1,0},{2,1},{3,2},{4,3},{5,4},{6,5},{7,6},{0,7},{9,8},{10,9},{11,1... | collective-permute-start | bytes 196616 | tf_op jit(solution)/shard_map/ppermute | solution.py:294
  44.5 0.5 collective-permute-start.16
  45.0 2.2 %collective-permute-done.12.refs_2_ = f32[32,512]{1,0:T(8,128)S(1)} collective-permute-done((f32[32,512]{1,0:T(8,128)S(1)}, f32[32,512]{1,0:T(8,128)S(1)}, u32[]{:S(2)}, u32[]{:S(2)}) %collective-permute-start.12) | collective-permute-done | bytes 65568 | tf_op jit(solution)/shard_map/ppermute | solution.py:294
  47.2 2.6 %collective-permute-start.13 = (f32[32,512]{1,0:T(8,128)S(1)}, f32[32,512]{1,0:T(8,128)S(1)}, u32[]{:S(2)}, u32[]{:S(2)}) collective-permute-start(f32[32,512]{1,0:T(8,128)S(1)} %collective-permute-done.12.refs_2_), channel_id=1, source_target_pairs={{1,0},{2,1},{3,2},{4,3},{5,4},{6,5},{7,6},{0,7},{9,8},{10,9},{11,1... | collective-permute-start | bytes 196616 | tf_op jit(solution)/shard_map/ppermute | solution.py:294
  49.9 1.8 %collective-permute-done.13.refs_3_ = f32[32,512]{1,0:T(8,128)S(1)} collective-permute-done((f32[32,512]{1,0:T(8,128)S(1)}, f32[32,512]{1,0:T(8,128)S(1)}, u32[]{:S(2)}, u32[]{:S(2)}) %collective-permute-start.13) | collective-permute-done | bytes 65568 | tf_op jit(solution)/shard_map/ppermute | solution.py:294
  51.7 3.6 %collective-permute-start.14 = (f32[32,512]{1,0:T(8,128)S(1)}, f32[32,512]{1,0:T(8,128)S(1)}, u32[]{:S(2)}, u32[]{:S(2)}) collective-permute-start(f32[32,512]{1,0:T(8,128)S(1)} %collective-permute-done.13.refs_3_), channel_id=1, source_target_pairs={{1,0},{2,1},{3,2},{4,3},{5,4},{6,5},{7,6},{0,7},{9,8},{10,9},{11,1... | collective-permute-start | bytes 196616 | tf_op jit(solution)/shard_map/ppermute | solution.py:312
  55.4 1.8 %collective-permute-done.14.refs_4_ = f32[32,512]{1,0:T(8,128)S(1)} collective-permute-done((f32[32,512]{1,0:T(8,128)S(1)}, f32[32,512]{1,0:T(8,128)S(1)}, u32[]{:S(2)}, u32[]{:S(2)}) %collective-permute-start.14) | collective-permute-done | bytes 65568 | tf_op jit(solution)/shard_map/ppermute | solution.py:312
  57.2 3.6 %collective-permute-start.18 = (f32[32,2048]{1,0:T(8,128)S(1)}, f32[32,2048]{1,0:T(8,128)S(1)}, u32[]{:S(2)}, u32[]{:S(2)}) collective-permute-start(f32[32,2048]{1,0:T(8,128)S(1)} %collective-permute-done.8.refs_2_), channel_id=1, source_target_pairs={{1,0},{2,1},{3,2},{4,3},{5,4},{6,5},{7,6},{0,7},{9,8},{10,9},{11,1... | collective-permute-start | bytes 786440 | tf_op jit(solution)/shard_map/ppermute | solution.py:294
  60.8 10.5 %early.1.state_ref = f32[256,512]{1,0:T(8,128)S(1)} custom-call(s32[4]{0:T(128)S(1)} %copy-done.1, f32[8,512]{1,0:T(8,128)S(1)} %slice.10.obs_ref, f32[32,512]{1,0:T(8,128)S(1)} %slice.11.refs_0_, f32[32,512]{1,0:T(8,128)S(1)} %collective-permute-done.11.refs_1_, f32[32,512]{1,0:T(8,128)S(1)} %collective-permute-done.12.refs_2_, ...), custom_call_target="tpu_custom_call" | custom-call | tf_op jit(solution)/shard_map/early/pallas_call | solution.py:236
  71.4 3.6 %collective-permute-start.20 = (f32[32,2048]{1,0:T(8,128)S(1)}, f32[32,2048]{1,0:T(8,128)S(1)}, u32[]{:S(2)}, u32[]{:S(2)}) collective-permute-start(f32[32,2048]{1,0:T(8,128)S(1)} %collective-permute-done.18.refs_3_), channel_id=1, source_target_pairs={{1,0},{2,1},{3,2},{4,3},{5,4},{6,5},{7,6},{0,7},{9,8},{10,9},{11,1... | collective-permute-start | bytes 786440 | tf_op jit(solution)/shard_map/ppermute | solution.py:316
  74.9 9.9 %late.1.mix_ref = f32[32,256]{1,0:T(8,128)S(1)} custom-call(s32[4]{0:T(128)S(1)} %copy-done.1, f32[8,512]{1,0:T(8,128)S(1)} %slice.10.obs_ref, f32[256,512]{1,0:T(8,128)S(1)} %early.1.state_ref), custom_call_target="tpu_custom_call" | custom-call | tf_op jit(solution)/shard_map/late/pallas_call | solution.py:236
  84.9 2.2 %update.1 = f32[32,2048]{1,0:T(8,128)} custom-call(f32[32,256]{1,0:T(8,128)S(1)} %late.1.mix_ref, f32[32,2048]{1,0:T(8,128)S(1)} %copy-done, f32[32,2048]{1,0:T(8,128)S(1)} %collective-permute-done.refs_1_, f32[32,2048]{1,0:T(8,128)S(1)} %collective-permute-done.8.refs_2_, f32[32,2048]{1,0:T(8,128)S(1)} %collective-permute-done.18.refs_3_, ...), custom_call_target="tpu_custom_call" | custom-call | tf_op jit(solution)/shard_map/update/pallas_call | solution.py:262
  (23 shorter events, 0.5 us)
Async XLA Ops:
  0.0 11.7 %collective-permute-start = (f32[32,2048]{1,0:T(8,128)}, f32[32,2048]{1,0:T(8,128)S(1)}, u32[]{:S(2)}, u32[]{:S(2)}) collective-permute-start(f32[32,2048]{1,0:T(8,128)} %refs_0_.1), channel_id=1, source_target_pairs={{1,0},{2,1},{3,2},{4,3},{5,4},{6,5},{7,6},{0,7},{9,8},{10,9},{11,1... | collective-permute-start | bytes 786440 | tf_op jit(solution)/shard_map/ppermute | solution.py:294
  5.9 9.2 %collective-permute-start.1 = (f32[32,2048]{1,0:T(8,128)}, f32[32,2048]{1,0:T(8,128)S(1)}, u32[]{:S(2)}, u32[]{:S(2)}) collective-permute-start(f32[32,2048]{1,0:T(8,128)} %refs_0_.1), channel_id=1, source_target_pairs={{7,0},{0,1},{1,2},{2,3},{3,4},{4,5},{5,6},{6,7},{15,8},{8,9},{9,10... | collective-permute-start | bytes 786440 | tf_op jit(solution)/shard_map/ppermute | solution.py:295
  15.0 5.4 %collective-permute-start.4 = (f32[40,512]{1,0:T(8,128)}, f32[40,512]{1,0:T(8,128)S(1)}, u32[]{:S(2)}, u32[]{:S(2)}) collective-permute-start(f32[40,512]{1,0:T(8,128)} %priors.1), channel_id=1, source_target_pairs={{0,192},{8,200},{16,208},{24,216},{32,224},{40,232},{48,240},{56,2... | collective-permute-start | bytes 245768 | tf_op jit(solution)/shard_map/ppermute | solution.py:305
  15.6 5.7 %collective-permute-start.3 = (f32[40,512]{1,0:T(8,128)}, f32[40,512]{1,0:T(8,128)S(1)}, u32[]{:S(2)}, u32[]{:S(2)}) collective-permute-start(f32[40,512]{1,0:T(8,128)} %priors.1), channel_id=1, source_target_pairs={{0,64},{8,72},{16,80},{24,88},{32,96},{40,104},{48,112},{56,120},{... | collective-permute-start | bytes 245768 | tf_op jit(solution)/shard_map/ppermute | solution.py:305
  17.1 6.2 %collective-permute-start.2 = (f32[40,512]{1,0:T(8,128)}, f32[40,512]{1,0:T(8,128)S(1)}, u32[]{:S(2)}, u32[]{:S(2)}) collective-permute-start(f32[40,512]{1,0:T(8,128)} %priors.1), channel_id=1, source_target_pairs={{0,128},{8,136},{16,144},{24,152},{32,160},{40,168},{48,176},{56,1... | collective-permute-start | bytes 245768 | tf_op jit(solution)/shard_map/ppermute | solution.py:305
  24.1 7.3 %collective-permute-start.7 = (f32[40,512]{1,0:T(8,128)S(1)}, f32[40,512]{1,0:T(8,128)S(1)}, u32[]{:S(2)}, u32[]{:S(2)}) collective-permute-start(f32[40,512]{1,0:T(8,128)S(1)} %add_add_fusion.1), channel_id=1, source_target_pairs={{0,48},{8,56},{16,0},{24,8},{32,16},{40,24},{48,32},{56,40},{64,11... | collective-permute-start | bytes 245768 | tf_op jit(solution)/shard_map/ppermute | solution.py:305
  27.2 6.5 %collective-permute-start.6 = (f32[40,512]{1,0:T(8,128)S(1)}, f32[40,512]{1,0:T(8,128)S(1)}, u32[]{:S(2)}, u32[]{:S(2)}) collective-permute-start(f32[40,512]{1,0:T(8,128)S(1)} %add_add_fusion.1), channel_id=1, source_target_pairs={{0,16},{8,24},{16,32},{24,40},{32,48},{40,56},{48,0},{56,8},{64,80... | collective-permute-start | bytes 245768 | tf_op jit(solution)/shard_map/ppermute | solution.py:305
  27.2 6.5 %collective-permute-start.5 = (f32[40,512]{1,0:T(8,128)S(1)}, f32[40,512]{1,0:T(8,128)S(1)}, u32[]{:S(2)}, u32[]{:S(2)}) collective-permute-start(f32[40,512]{1,0:T(8,128)S(1)} %add_add_fusion.1), channel_id=1, source_target_pairs={{0,32},{8,40},{16,48},{24,56},{32,0},{40,8},{48,16},{56,24},{64,96... | collective-permute-start | bytes 245768 | tf_op jit(solution)/shard_map/ppermute | solution.py:305
  29.4 6.4 %collective-permute-start.8 = (f32[32,2048]{1,0:T(8,128)S(1)}, f32[32,2048]{1,0:T(8,128)S(1)}, u32[]{:S(2)}, u32[]{:S(2)}) collective-permute-start(f32[32,2048]{1,0:T(8,128)S(1)} %collective-permute-done.refs_1_), channel_id=1, source_target_pairs={{1,0},{2,1},{3,2},{4,3},{5,4},{6,5},{7,6},{0,7},{9,8},{10,9},{11,1... | collective-permute-start | bytes 786440 | tf_op jit(solution)/shard_map/ppermute | solution.py:294
  29.7 7.6 %collective-permute-start.9 = (f32[32,2048]{1,0:T(8,128)S(1)}, f32[32,2048]{1,0:T(8,128)S(1)}, u32[]{:S(2)}, u32[]{:S(2)}) collective-permute-start(f32[32,2048]{1,0:T(8,128)S(1)} %collective-permute-done.1.refs_7_), channel_id=1, source_target_pairs={{7,0},{0,1},{1,2},{2,3},{3,4},{4,5},{5,6},{6,7},{15,8},{8,9},{9,10... | collective-permute-start | bytes 786440 | tf_op jit(solution)/shard_map/ppermute | solution.py:295
  37.3 1.3 %collective-permute-start.10 = (f32[40,512]{1,0:T(8,128)S(1)}, f32[40,512]{1,0:T(8,128)S(1)}, u32[]{:S(2)}, u32[]{:S(2)}) collective-permute-start(f32[40,512]{1,0:T(8,128)S(1)} %add_add_fusion), channel_id=1, source_target_pairs={{0,8},{8,0},{16,24},{24,16},{32,40},{40,32},{48,56},{56,48},{64,72... | collective-permute-start | bytes 245768 | tf_op jit(solution)/shard_map/ppermute | solution.py:308
  38.6 22.2 %copy-start.1 = (s32[4]{0:T(128)S(1)}, s32[4]{0:T(128)}, u32[]{:S(2)}) copy-start(s32[4]{0:T(128)} %counts_ref.3) | copy-start | bytes 52
  38.6 4.3 %collective-permute-start.11 = (f32[32,512]{1,0:T(8,128)S(1)}, f32[32,512]{1,0:T(8,128)S(1)}, u32[]{:S(2)}, u32[]{:S(2)}) collective-permute-start(f32[32,512]{1,0:T(8,128)S(1)} %slice.11.refs_0_), channel_id=1, source_target_pairs={{1,0},{2,1},{3,2},{4,3},{5,4},{6,5},{7,6},{0,7},{9,8},{10,9},{11,1... | collective-permute-start | bytes 196616 | tf_op jit(solution)/shard_map/ppermute | solution.py:294
  38.7 5.7 %collective-permute-start.15 = (f32[32,512]{1,0:T(8,128)S(1)}, f32[32,512]{1,0:T(8,128)S(1)}, u32[]{:S(2)}, u32[]{:S(2)}) collective-permute-start(f32[32,512]{1,0:T(8,128)S(1)} %slice.11.refs_0_), channel_id=1, source_target_pairs={{7,0},{0,1},{1,2},{2,3},{3,4},{4,5},{5,6},{6,7},{15,8},{8,9},{9,10... | collective-permute-start | bytes 196616 | tf_op jit(solution)/shard_map/ppermute | solution.py:295
  43.0 4.3 %collective-permute-start.12 = (f32[32,512]{1,0:T(8,128)S(1)}, f32[32,512]{1,0:T(8,128)S(1)}, u32[]{:S(2)}, u32[]{:S(2)}) collective-permute-start(f32[32,512]{1,0:T(8,128)S(1)} %collective-permute-done.11.refs_1_), channel_id=1, source_target_pairs={{1,0},{2,1},{3,2},{4,3},{5,4},{6,5},{7,6},{0,7},{9,8},{10,9},{11,1... | collective-permute-start | bytes 196616 | tf_op jit(solution)/shard_map/ppermute | solution.py:294
  44.5 5.5 %collective-permute-start.16 = (f32[32,512]{1,0:T(8,128)S(1)}, f32[32,512]{1,0:T(8,128)S(1)}, u32[]{:S(2)}, u32[]{:S(2)}) collective-permute-start(f32[32,512]{1,0:T(8,128)S(1)} %collective-permute-done.15.refs_7_), channel_id=1, source_target_pairs={{7,0},{0,1},{1,2},{2,3},{3,4},{4,5},{5,6},{6,7},{15,8},{8,9},{9,10... | collective-permute-start | bytes 196616 | tf_op jit(solution)/shard_map/ppermute | solution.py:295
  47.2 4.5 %collective-permute-start.13 = (f32[32,512]{1,0:T(8,128)S(1)}, f32[32,512]{1,0:T(8,128)S(1)}, u32[]{:S(2)}, u32[]{:S(2)}) collective-permute-start(f32[32,512]{1,0:T(8,128)S(1)} %collective-permute-done.12.refs_2_), channel_id=1, source_target_pairs={{1,0},{2,1},{3,2},{4,3},{5,4},{6,5},{7,6},{0,7},{9,8},{10,9},{11,1... | collective-permute-start | bytes 196616 | tf_op jit(solution)/shard_map/ppermute | solution.py:294
  49.9 5.5 %collective-permute-start.17 = (f32[32,512]{1,0:T(8,128)S(1)}, f32[32,512]{1,0:T(8,128)S(1)}, u32[]{:S(2)}, u32[]{:S(2)}) collective-permute-start(f32[32,512]{1,0:T(8,128)S(1)} %collective-permute-done.16.refs_6_), channel_id=1, source_target_pairs={{7,0},{0,1},{1,2},{2,3},{3,4},{4,5},{5,6},{6,7},{15,8},{8,9},{9,10... | collective-permute-start | bytes 196616 | tf_op jit(solution)/shard_map/ppermute | solution.py:295
  51.7 5.5 %collective-permute-start.14 = (f32[32,512]{1,0:T(8,128)S(1)}, f32[32,512]{1,0:T(8,128)S(1)}, u32[]{:S(2)}, u32[]{:S(2)}) collective-permute-start(f32[32,512]{1,0:T(8,128)S(1)} %collective-permute-done.13.refs_3_), channel_id=1, source_target_pairs={{1,0},{2,1},{3,2},{4,3},{5,4},{6,5},{7,6},{0,7},{9,8},{10,9},{11,1... | collective-permute-start | bytes 196616 | tf_op jit(solution)/shard_map/ppermute | solution.py:312
  57.2 14.1 %collective-permute-start.18 = (f32[32,2048]{1,0:T(8,128)S(1)}, f32[32,2048]{1,0:T(8,128)S(1)}, u32[]{:S(2)}, u32[]{:S(2)}) collective-permute-start(f32[32,2048]{1,0:T(8,128)S(1)} %collective-permute-done.8.refs_2_), channel_id=1, source_target_pairs={{1,0},{2,1},{3,2},{4,3},{5,4},{6,5},{7,6},{0,7},{9,8},{10,9},{11,1... | collective-permute-start | bytes 786440 | tf_op jit(solution)/shard_map/ppermute | solution.py:294
  60.8 10.6 %collective-permute-start.19 = (f32[32,2048]{1,0:T(8,128)S(1)}, f32[32,2048]{1,0:T(8,128)S(1)}, u32[]{:S(2)}, u32[]{:S(2)}) collective-permute-start(f32[32,2048]{1,0:T(8,128)S(1)} %collective-permute-done.9.refs_6_), channel_id=1, source_target_pairs={{7,0},{0,1},{1,2},{2,3},{3,4},{4,5},{5,6},{6,7},{15,8},{8,9},{9,10... | collective-permute-start | bytes 786440 | tf_op jit(solution)/shard_map/ppermute | solution.py:295
  71.3 13.5 %copy-start = (f32[32,2048]{1,0:T(8,128)S(1)}, f32[32,2048]{1,0:T(8,128)}, u32[]{:S(2)}) copy-start(f32[32,2048]{1,0:T(8,128)} %refs_0_.1) | copy-start | bytes 786436
  71.4 13.5 %collective-permute-start.20 = (f32[32,2048]{1,0:T(8,128)S(1)}, f32[32,2048]{1,0:T(8,128)S(1)}, u32[]{:S(2)}, u32[]{:S(2)}) collective-permute-start(f32[32,2048]{1,0:T(8,128)S(1)} %collective-permute-done.18.refs_3_), channel_id=1, source_target_pairs={{1,0},{2,1},{3,2},{4,3},{5,4},{6,5},{7,6},{0,7},{9,8},{10,9},{11,1... | collective-permute-start | bytes 786440 | tf_op jit(solution)/shard_map/ppermute | solution.py:316
